TPU v7x, 128 devices: a whole 4x4x4 slice. The times are simulated.
128 devices in a mesh: dp: 16 (over y, z), expert: 8 (over x, core).
Axes of the slice: x: 4, y: 4, z: 4, core: 2. Of those that a mesh axis runs over, the one named last changes fastest.
Arguments:
- grad_out: bfloat16 [16384, 6144], P(('dp', 'expert')), may hold values from -6 to 6
- routes: int32 [16384, 2], P(('dp', 'expert')), may hold values from 0 to 31, all different within a row; in each aligned block of 128 rows (0 to 127, 128 to 255, ...) at most 9 rows name the same one
- loss_weight: int32 [16384], P(('dp', 'expert')), may hold values from 1 to 4
- saved_input: bfloat16 [32, 1152, 6144], P('dp', None, 'expert'), may hold values from -6 to 6
- saved_gate: bfloat16 [32, 1152, 1024], P('dp', None, 'expert'), may hold values from -8 to 8
- saved_up: bfloat16 [32, 1152, 1024], P('dp', None, 'expert'), may hold values from -6 to 6
- w_gate: bfloat16 [32, 6144, 1024], P('dp', 'expert'), may hold values from -0.1875 to 0.1875
- w_up: bfloat16 [32, 6144, 1024], P('dp', 'expert'), may hold values from -0.1875 to 0.1875
- w_down: bfloat16 [32, 1024, 6144], P('dp', None, 'expert'), may hold values from -0.078125 to 0.078125
Outputs:
- grad_input: bfloat16 [16384, 6144], P(('dp', 'expert'))
- grad_gate: bfloat16 [32, 6144, 1024], P('dp', 'expert')
- grad_up: bfloat16 [32, 6144, 1024], P('dp', 'expert')
- grad_down: bfloat16 [32, 1024, 6144], P('dp', None, 'expert')
Inputs may be any that keep to these rules, and one draw needn't show every extreme that they name: `routes`: each row names two different experts; among the rows of one device no expert is named more than 9 times, and some device names some expert exactly 9 times.
All inputs are finite; a program needn't handle non-finite values.
Results may differ from a plain program's by a relative error of at most 0.0061.
Values may be sent and summed in bfloat16 or wider, within the bound.
No kernel may reach another device: no remote copies, remote signals or barrier semaphores. Data moves between devices by JAX's collectives and lax.ppermute only.
A program may use at most 192 MiB of HBM per device.

v0:
```python
import jax
import jax.numpy as jnp
from jax import lax
from jax.sharding import PartitionSpec as P


def body(grad_out, routes, loss_weight, saved_input, saved_gate, saved_up, w_gate, w_up, w_down):
    groups = lax.axis_size("dp")
    splits = lax.axis_size("expert")
    local_experts = w_gate.shape[0]
    experts_all = local_experts * groups
    tokens_here = grad_out.shape[0]
    width = grad_out.shape[1]
    slice_width = width // splits
    slots_all = saved_input.shape[1]
    capacity = slots_all // (groups * splits)
    scaled = (
        grad_out.astype(jnp.float32) * loss_weight.astype(jnp.float32)[:, None] * 0.25
    ).astype(jnp.bfloat16)
    chosen = routes.reshape(-1)
    onehot = (chosen[:, None] == jnp.arange(experts_all, dtype=jnp.int32)[None, :]).astype(
        jnp.int32
    )
    before = jnp.cumsum(onehot, axis=0) - onehot
    rank = jnp.sum(before * onehot, axis=1)
    dest_row = (chosen % local_experts * groups + chosen // local_experts) * capacity + rank
    marks = (
        dest_row[:, None] == jnp.arange(experts_all * capacity, dtype=jnp.int32)[None, :]
    ).astype(jnp.float32)
    placed = jnp.sum(marks.reshape(tokens_here, 2, experts_all * capacity), axis=1).astype(
        jnp.bfloat16
    )
    outgoing = jnp.einsum("tr,td->rd", placed, scaled, preferred_element_type=jnp.float32).astype(
        jnp.bfloat16
    )
    ordered = outgoing.reshape(local_experts, groups, capacity, splits, slice_width)
    ordered = ordered.transpose(0, 1, 3, 2, 4).reshape(
        local_experts, groups * splits, capacity, slice_width
    )
    arrived = lax.all_to_all(ordered, ("dp", "expert"), split_axis=1, concat_axis=1, tiled=True)
    dispatched = arrived.reshape(local_experts, slots_all, slice_width)
    partial_value = jnp.einsum(
        "esd,ehd->esh", dispatched, w_down, preferred_element_type=jnp.float32
    )
    dhidden = lax.psum(partial_value, "expert")
    gates_all, ups_all = (
        lax.all_gather(saved_gate, "expert", axis=2, tiled=True),
        lax.all_gather(saved_up, "expert", axis=2, tiled=True),
    )
    gvals = gates_all.astype(jnp.float32)
    uvals = ups_all.astype(jnp.float32)
    sig = jax.nn.sigmoid(gvals)
    act = gvals * sig
    hidden = (act * uvals).astype(jnp.bfloat16)
    dgate = (dhidden * uvals * sig * (1.0 + gvals * (1.0 - sig))).astype(jnp.bfloat16)
    dup = (dhidden * act).astype(jnp.bfloat16)
    hidden, dgate, dup = (hidden, dgate, dup)
    grad_down = jnp.einsum(
        "esh,esd->ehd", hidden, dispatched, preferred_element_type=jnp.float32
    ).astype(jnp.bfloat16)
    grad_gate = jnp.einsum(
        "esd,esh->edh", saved_input, dgate, preferred_element_type=jnp.float32
    ).astype(jnp.bfloat16)
    grad_up = jnp.einsum(
        "esd,esh->edh", saved_input, dup, preferred_element_type=jnp.float32
    ).astype(jnp.bfloat16)
    slot_grad = jnp.einsum("esh,edh->esd", dgate, w_gate, preferred_element_type=jnp.float32)
    slot_grad = slot_grad + jnp.einsum(
        "esh,edh->esd", dup, w_up, preferred_element_type=jnp.float32
    )
    slot_grad = slot_grad.astype(jnp.bfloat16)
    leaving = slot_grad.reshape(local_experts, groups * splits, capacity, slice_width)
    returned = lax.all_to_all(leaving, ("dp", "expert"), split_axis=1, concat_axis=1, tiled=True)
    returned = returned.reshape(local_experts, groups, splits, capacity, slice_width).transpose(
        0, 1, 3, 2, 4
    )
    returned = returned.reshape(experts_all * capacity, width)
    grad_input = jnp.einsum(
        "tr,rd->td", placed, returned, preferred_element_type=jnp.float32
    ).astype(jnp.bfloat16)
    return (grad_input, grad_gate, grad_up, grad_down)


def solution(mesh):
    return jax.shard_map(
        body,
        mesh=mesh,
        in_specs=(
            P(("dp", "expert"), None),
            P(("dp", "expert"), None),
            P(("dp", "expert")),
            P("dp", None, "expert"),
            P("dp", None, "expert"),
            P("dp", None, "expert"),
            P("dp", "expert", None),
            P("dp", "expert", None),
            P("dp", None, "expert"),
        ),
        out_specs=(
            P(("dp", "expert"), None),
            P("dp", "expert", None),
            P("dp", "expert", None),
            P("dp", None, "expert"),
        ),
        check_vma=False,
    )
```

profile of v0, /device:TPU:1, one launch (start us, length us, event | category | flops | bytes accessed | tf_op | source)
XLA Modules:
  0.0 385.4 jit_solution(1867682180642988697)
XLA Ops:
  7.2 0.0 copy-start
  7.2 0.0 all-reduce.2.cloned.1.call-start
  7.2 1.6 copy.105
  8.8 1.0 eq.45
  9.8 1.0 eq.41
  10.7 0.7 convert_element_type.67
  11.4 0.6 fusion.25
  12.0 1.9 reduce-window.6
  13.9 0.9 slice_reduce_fusion
  14.9 0.9 fusion.24
  15.8 0.8 reduce_sum.21
  16.5 0.9 copy.108
  17.4 0.7 multiply_add_fusion
  18.2 0.0 copy-start.4
  18.2 2.6 convolution_convert_fusion
  20.8 0.0 copy-done.4
  20.8 1.0 copy.124
  21.8 0.4 copy.134
  22.3 3.6 copy.110
  25.9 0.0 copy-start.6
  25.9 57.3 %all_to_all.10 = bf16[2,128,9,768]{3,0,2,1:T(2,128)(2,1)S(1)} all-to-all(bf16[2,128,9,768]{3,0,2,1:T(2,128)(2,1)S(1)} %copy.110), channel_id=1, replica_groups=mesh['dp'=16,'expert'=8] {'dp','expert'}, dimensions={1} | all-to-all | bytes 7077888 | tf_op jit(solution)/shard_map/all_to_all | solution.py:40
  83.2 0.0 copy-start.3
  83.3 1.9 copy-done.3
  85.1 0.0 copy-done.6
  85.1 6.2 %fusion.11 = f32[2,1152,1024]{2,1,0:T(8,128)} fusion(bf16[2,1024,768]{2,1,0:T(8,128)(2,1)S(1)} %copy-done.6, bf16[2,1152,768]{2,0,1:T(2,128)(2,1)S(1)} %bitcast.56), kind=kOutput, calls=%fused_computation.23 | convolution fusion | flops 3623878656 | bytes 16121856 | tf_op jit(solution)/shard_map/esd,ehd->esh/dot_general | solution.py:42
  91.3 0.0 all-reduce.2.cloned.1.call-update
  91.3 0.0 all-gather.5.cloned.1.call-start
  91.4 0.7 all-gather.5.cloned.1.call-update
  92.1 0.2 all-gather.3.cloned.1.call-start
  92.3 0.5 all-gather.3.cloned.1.call-update
  92.8 108.4 %all-reduce.2.cloned.1.call-done = f32[2,1152,1024]{2,1,0:T(8,128)} async-done(((f32[2,1152,1024]{2,1,0:T(8,128)}), f32[2,1152,1024]{2,1,0:T(8,128)}) %all-reduce.2.cloned.1.call-update) | async-done | bytes 9437200 | tf_op jit(solution)/shard_map/psum | solution.py:45
  201.2 40.5 %all-gather.5.cloned.1.call-done = bf16[2,1152,1024]{2,1,0:T(8,128)(2,1)} async-done(((bf16[2,1152,128]{2,1,0:T(8,128)(2,1)}), bf16[2,1152,1024]{2,1,0:T(8,128)(2,1)}) %all-gather.5.cloned.1.call-update) | async-done | bytes 4718608 | tf_op jit(solution)/shard_map/all_gather | solution.py:47
  241.8 41.0 %all-gather.3.cloned.1.call-done = bf16[2,1152,1024]{2,1,0:T(8,128)(2,1)} async-done(((bf16[2,1152,128]{2,1,0:T(8,128)(2,1)}), bf16[2,1152,1024]{2,1,0:T(8,128)(2,1)}) %all-gather.3.cloned.1.call-update) | async-done | bytes 4718608 | tf_op jit(solution)/shard_map/all_gather | solution.py:48
  282.7 0.0 copy-start.7
  282.7 9.0 %multiply_convert_fusion = (bf16[2,1152,1024]{2,1,0:T(8,128)(2,1)S(1)}, bf16[2,1152,1024]{2,1,0:T(8,128)(2,1)S(1)}) fusion(f32[2,1152,1024]{2,1,0:T(8,128)} %all-reduce.2.cloned.1.call-done, bf16[2,1152,1024]{2,1,0:T(8,128)(2,1)} %all-gather.5.cloned.1.call-done, bf16[2,1152,1024]{2,1,0:T(8,128)(2,1)} %all-gather.3.cloned.1.call-done), kind=kLoop, calls=%fused_computation.13 | loop fusion | flops 35389440 | bytes 28311552 | tf_op jit(solution)/shard_map/convert_element_type | solution.py:56
  291.8 0.0 copy-start.1
  291.8 0.0 copy-start.2
  291.8 0.0 copy-done.7
  291.8 0.0 copy-start.8
  291.8 5.9 %fusion.30 = f32[2,1152,768]{2,1,0:T(8,128)} fusion(bf16[2,1152,1024]{2,1,0:T(8,128)(2,1)S(1)} %get-tuple-element.29, bf16[2,768,1024]{2,1,0:T(8,128)(2,1)S(1)} %copy-done.7), kind=kOutput, calls=%fused_computation.51 | convolution fusion | flops 3623878656 | bytes 14942208 | tf_op jit(solution)/shard_map/esh,edh->esd/dot_general | solution.py:67
  297.8 0.0 copy-done.1
  297.8 0.4 copy-done.2
  298.2 0.0 copy-done.8
  298.2 6.1 %add_convert_fusion = bf16[2,1152,768]{2,1,0:T(8,128)(2,1)S(1)} fusion(f32[2,1152,768]{2,1,0:T(8,128)} %fusion.30, bf16[2,1152,1024]{2,1,0:T(8,128)(2,1)S(1)} %get-tuple-element.28, bf16[2,768,1024]{2,1,0:T(8,128)(2,1)S(1)} %copy-done.8), kind=kOutput, calls=%fused_computation.16 | convolution fusion | flops 3627417600 | bytes 18481152 | tf_op jit(solution)/shard_map/esh,edh->esd/dot_general | solution.py:68
  304.3 13.9 %copy.112 = bf16[2,1152,768]{2,0,1:T(2,128)(2,1)} copy(bf16[2,1152,768]{2,1,0:T(8,128)(2,1)S(1)} %add_convert_fusion) | data formatting | bytes 7077888 | tf_op jit(solution)/shard_map/convert_element_type | solution.py:71
  318.2 9.3 %all-to-all-start.1 = ((bf16[2,128,9,768]{3,0,2,1:T(2,128)(2,1)}), bf16[2,128,9,768]{3,0,2,1:T(2,128)(2,1)}, u32[]{:S(2)}, u32[]{:S(2)}) async-start(bf16[2,128,9,768]{3,0,2,1:T(2,128)(2,1)} %bitcast.52), calls=%async_computation.1 | async-start | bytes 7077888 | tf_op jit(solution)/shard_map/all_to_all | solution.py:73
  327.5 0.0 copy-done
  327.5 9.4 %convert_bitcast_fusion = bf16[2,768,1024]{1,2,0:T(8,128)(2,1)} fusion(bf16[2,1152,1024]{2,1,0:T(8,128)(2,1)} %copy-done.2, bf16[2,1152,768]{2,1,0:T(8,128)(2,1)S(1)} %copy-done), kind=kOutput, calls=%fused_computation.19 | convolution fusion | flops 3625451520 | bytes 11403264 | tf_op jit(solution)/shard_map/esd,esh->edh/dot_general | solution.py:64
  337.0 4.6 %copy.119 = bf16[2,768,1024]{2,1,0:T(8,128)(2,1)} copy(bf16[2,768,1024]{1,2,0:T(8,128)(2,1)} %convert_bitcast_fusion) | data formatting | bytes 6291456
  341.6 9.4 %convert_bitcast_fusion.1 = bf16[2,768,1024]{1,2,0:T(8,128)(2,1)} fusion(bf16[2,1152,1024]{2,1,0:T(8,128)(2,1)} %copy-done.1, bf16[2,1152,768]{2,1,0:T(8,128)(2,1)S(1)} %copy-done), kind=kOutput, calls=%fused_computation.20 | convolution fusion | flops 3625451520 | bytes 11403264 | tf_op jit(solution)/shard_map/esd,esh->edh/dot_general | solution.py:61
  351.0 4.6 %copy.118 = bf16[2,768,1024]{2,1,0:T(8,128)(2,1)} copy(bf16[2,768,1024]{1,2,0:T(8,128)(2,1)} %convert_bitcast_fusion.1) | data formatting | bytes 6291456
  355.6 12.1 %fusion.13 = bf16[2,1024,768]{2,1,0:T(8,128)(2,1)} fusion(bf16[2,1152,768]{2,0,1:T(2,128)(2,1)} %bitcast.57, bf16[2,1152,1024]{2,1,0:T(8,128)(2,1)} %all-gather.3.cloned.1.call-done, bf16[2,1152,1024]{2,1,0:T(8,128)(2,1)} %all-gather.5.cloned.1.call-done), kind=kOutput, calls=%fused_computation.25 | convolution fusion | flops 3644325888 | bytes 16121856 | tf_op jit(solution)/shard_map/esh,esd->ehd/dot_general | solution.py:58
  367.8 5.5 %all-to-all-done.1 = bf16[2,128,9,768]{3,0,2,1:T(2,128)(2,1)} async-done(((bf16[2,128,9,768]{3,0,2,1:T(2,128)(2,1)}), bf16[2,128,9,768]{3,0,2,1:T(2,128)(2,1)}, u32[]{:S(2)}, u32[]{:S(2)}) %all-to-all-start.1) | async-done | bytes 3538976 | tf_op jit(solution)/shard_map/all_to_all | solution.py:73
  373.2 2.5 copy.113
  375.7 0.0 copy-start.5
  375.7 1.0 copy.125
  376.7 0.0 copy-done.5
  376.7 2.2 convolution_convert_fusion.1
  (3 shorter events, 0.1 us)
Async XLA Ops:
  7.2 320.4 %copy-start = (bf16[2,1152,768]{2,1,0:T(8,128)(2,1)S(1)}, bf16[2,1152,768]{2,1,0:T(8,128)(2,1)}, u32[]{:S(2)}) copy-start(bf16[2,1152,768]{2,1,0:T(8,128)(2,1)} %param.12) | copy-start | bytes 10616836
  7.2 194.1 %all-reduce.2.cloned.1.call-start = ((), (), s32[]{:S(2)}) async-start(), calls=%async_computation.2 | async-start | bytes 18874368 | tf_op jit(solution)/shard_map/psum | solution.py:45
  18.2 2.6 copy-start.4
  25.9 59.2 %copy-start.6 = (bf16[2,1024,768]{2,1,0:T(8,128)(2,1)S(1)}, bf16[2,1024,768]{2,1,0:T(8,128)(2,1)}, u32[]{:S(2)}) copy-start(bf16[2,1024,768]{2,1,0:T(8,128)(2,1)} %param.17) | copy-start | bytes 9437188
  83.2 1.9 copy-start.3
  91.3 150.4 %all-gather.5.cloned.1.call-start = ((), (), s32[]{:S(2)}) async-start(), calls=%async_computation.4 | async-start | bytes 5308416 | tf_op jit(solution)/shard_map/all_gather | solution.py:47
  92.1 190.6 %all-gather.3.cloned.1.call-start = ((), (), s32[]{:S(2)}) async-start(), calls=%async_computation.3 | async-start | bytes 5308416 | tf_op jit(solution)/shard_map/all_gather | solution.py:48
  282.7 9.1 %copy-start.7 = (bf16[2,768,1024]{2,1,0:T(8,128)(2,1)S(1)}, bf16[2,768,1024]{2,1,0:T(8,128)(2,1)}, u32[]{:S(2)}) copy-start(bf16[2,768,1024]{2,1,0:T(8,128)(2,1)} %param.15) | copy-start | bytes 9437188
  291.8 6.0 %copy-start.1 = (bf16[2,1152,1024]{2,1,0:T(8,128)(2,1)}, bf16[2,1152,1024]{2,1,0:T(8,128)(2,1)S(1)}, u32[]{:S(2)}) copy-start(bf16[2,1152,1024]{2,1,0:T(8,128)(2,1)S(1)} %get-tuple-element.29) | copy-start | bytes 14155780
  291.8 6.4 %copy-start.2 = (bf16[2,1152,1024]{2,1,0:T(8,128)(2,1)}, bf16[2,1152,1024]{2,1,0:T(8,128)(2,1)S(1)}, u32[]{:S(2)}) copy-start(bf16[2,1152,1024]{2,1,0:T(8,128)(2,1)S(1)} %get-tuple-element.28) | copy-start | bytes 14155780
  291.8 6.4 %copy-start.8 = (bf16[2,768,1024]{2,1,0:T(8,128)(2,1)S(1)}, bf16[2,768,1024]{2,1,0:T(8,128)(2,1)}, u32[]{:S(2)}) copy-start(bf16[2,768,1024]{2,1,0:T(8,128)(2,1)} %param.16) | copy-start | bytes 9437188
  318.2 55.0 %all-to-all-start.1 = ((bf16[2,128,9,768]{3,0,2,1:T(2,128)(2,1)}), bf16[2,128,9,768]{3,0,2,1:T(2,128)(2,1)}, u32[]{:S(2)}, u32[]{:S(2)}) async-start(bf16[2,128,9,768]{3,0,2,1:T(2,128)(2,1)} %bitcast.52), calls=%async_computation.1 | async-start | bytes 7077888 | tf_op jit(solution)/shard_map/all_to_all | solution.py:73
  375.7 1.0 copy-start.5
Sparse Core Ops, SparseCore 0:
  91.5 109.7 all-reduce.1
  202.9 38.8 all-gather.4
  243.5 39.2 all-gather.2
where the time goes:
time: 386 us; the launch traced here: 385 us
  waiting for transfers between devices  197 us (51%)
  blocking collectives  57.3 us (15%)
  matrix products  54 us (14%)
  local copies, waits for them, and re-layouts  40.1 us (10%)
  other arithmetic  13.9 us (4%)
  between operations  13.9 us (4%)
  starting transfers between devices  9.56 us (2%)
    psum x1, waiting for transfers between devices, body(): dhidden = lax.psum(partial_value, 'expert')  108 us
    all_to_all x1, blocking collectives, body(): lax.all_to_all(ordered, ('dp', 'expert'), split_axis=1, concat_axis=1, ti...  57.3 us
    all_gather x1, waiting for transfers between devices, body(): lax.all_gather(saved_up, 'expert', axis=2, tiled=True)  41 us
    all_gather x1, waiting for transfers between devices, body(): lax.all_gather(saved_gate, 'expert', axis=2, tiled=True)  40.5 us
    unnamed x23, local copies, waits for them, and re-layouts  15.2 us
    convert_element_type x1, local copies, waits for them, and re-layouts, body(): slot_grad = slot_grad.astype(jnp.bfloat16)  13.9 us
    dot_general x1, matrix products, body(): jnp.einsum('esh,esd->ehd', hidden, dispatched, preferred_element_type=jnp...  12.1 us
    dot_general x1, matrix products, body(): jnp.einsum('esd,esh->edh', saved_input, dup, preferred_element_type=jnp.f...  9.43 us
  transfers between devices with their start and end apart: 4, of which 4 were waited for; matrix products, arithmetic and copies ran while one was open for 10% of the time, Pallas kernels for 0%

commit v1 on v0

--- a/solution.py
+++ b/solution.py
@@ -2,6 +2,19 @@
 import jax.numpy as jnp
 from jax import lax
 from jax.sharding import PartitionSpec as P
+
+
+def ring_gather(x, axis, dim):
+    ways = lax.axis_size(axis)
+    up = [(d, (d + 1) % ways) for d in range(ways)]
+    down = [(d, (d - 1) % ways) for d in range(ways)]
+    earlier, later = ([x], [x])
+    for _ in range(ways // 2):
+        earlier.append(lax.ppermute(earlier[-1], axis, up))
+    for _ in range((ways - 1) // 2):
+        later.append(lax.ppermute(later[-1], axis, down))
+    line = jnp.concatenate([*earlier[::-1], *later[1:]], axis=dim)
+    return jnp.roll(line, (lax.axis_index(axis) - ways // 2) * x.shape[dim], axis=dim)
 
 
 def body(grad_out, routes, loss_weight, saved_input, saved_gate, saved_up, w_gate, w_up, w_down):
@@ -45,7 +58,7 @@
     dhidden = lax.psum(partial_value, "expert")
     gates_all, ups_all = (
         lax.all_gather(saved_gate, "expert", axis=2, tiled=True),
-        lax.all_gather(saved_up, "expert", axis=2, tiled=True),
+        ring_gather(saved_up, "expert", 2),
     )
     gvals = gates_all.astype(jnp.float32)
     uvals = ups_all.astype(jnp.float32)

time: 386 us -> 365 us (0.946)
  waiting for transfers between devices: 197 us -> 132 us
  local copies, waits for them, and re-layouts: 40.1 us -> 68.4 us
  starting transfers between devices: 9.56 us -> 23.5 us
    psum x1, waiting for transfers between devices: 108 us -> 39.7 us  [body(): dhidden = lax.psum(partial_value, 'expert')]
    ppermute x0 -> x7, waiting for transfers between devices: none -> 46.1 us  [the longest x4 45.6 us: ring_gather(): earlier.append(lax.ppermute(earlier[-1], axis, up))]
    all_gather x1 -> x0, waiting for transfers between devices: 41 us -> none  [body(): lax.all_gather(saved_up, 'expert', axis=2, tiled=True)]
    unnamed x23 -> x48, local copies, waits for them, and re-layouts: 15.2 us -> 42.5 us
    ppermute x0 -> x7, starting transfers between devices: none -> 13.9 us  [the longest x4 8.51 us: ring_gather(): earlier.append(lax.ppermute(earlier[-1], axis, up))]
  transfers between devices with their start and end apart: 4 -> 10, of which waited for: 4 -> 8; matrix products, arithmetic and copies ran while one was open for 10% -> 18% of each run, Pallas kernels for 0% -> 0%
where the time goes in v1:
time: 365 us; the launch traced here: 364 us
  waiting for transfers between devices  132 us (36%)
  local copies, waits for them, and re-layouts  68.4 us (19%)
  blocking collectives  57.3 us (16%)
  matrix products  54 us (15%)
  starting transfers between devices  23.5 us (6%)
  between operations  14.2 us (4%)
  other arithmetic  13.9 us (4%)
    all_to_all x1, blocking collectives, body(): lax.all_to_all(ordered, ('dp', 'expert'), split_axis=1, concat_axis=1, ti...  57.3 us
    ppermute x4, waiting for transfers between devices, ring_gather(): earlier.append(lax.ppermute(earlier[-1], axis, up))  45.6 us
    unnamed x48, local copies, waits for them, and re-layouts  42.5 us
    all_gather x1, waiting for transfers between devices, body(): lax.all_gather(saved_gate, 'expert', axis=2, tiled=True)  40.5 us
    psum x1, waiting for transfers between devices, body(): dhidden = lax.psum(partial_value, 'expert')  39.7 us
    convert_element_type x1, local copies, waits for them, and re-layouts, body(): slot_grad = slot_grad.astype(jnp.bfloat16)  14 us
    dot_general x1, matrix products, body(): jnp.einsum('esh,esd->ehd', hidden, dispatched, preferred_element_type=jnp...  12.1 us
    dot_general x1, matrix products, body(): jnp.einsum('esd,esh->edh', saved_input, dgate, preferred_element_type=jnp...  9.43 us
  transfers between devices with their start and end apart: 10, of which 8 were waited for; matrix products, arithmetic and copies ran while one was open for 18% of the time, Pallas kernels for 0%

profile of v1, /device:TPU:1, one launch (start us, length us, event | category | flops | bytes accessed | tf_op | source)
XLA Modules:
  0.0 363.7 jit_solution(3476524283738627004)
XLA Ops:
  7.2 1.6 copy.105
  8.8 1.0 eq.48
  9.8 1.0 eq.44
  10.7 0.6 fusion.26
  11.4 1.9 reduce-window.6
  13.3 0.9 slice_reduce_fusion
  14.2 0.9 fusion.25
  15.1 0.8 reduce_sum.21
  15.9 0.9 copy.108
  16.8 0.7 multiply_add_fusion
  17.5 0.7 convert_element_type.67
  18.2 2.6 convolution_convert_fusion
  20.8 1.0 copy.124
  22.3 3.6 %copy.110 = bf16[2,128,9,768]{3,0,2,1:T(2,128)(2,1)S(1)} copy(bf16[2,128,9,768]{3,1,2,0:T(8,128)(2,1)S(1)} %bitcast.54) | data formatting | bytes 7077888 | tf_op jit(solution)/shard_map/reshape | solution.py:50
  25.9 57.3 %all_to_all.10 = bf16[2,128,9,768]{3,0,2,1:T(2,128)(2,1)S(1)} all-to-all(bf16[2,128,9,768]{3,0,2,1:T(2,128)(2,1)S(1)} %copy.110), channel_id=1, replica_groups=mesh['dp'=16,'expert'=8] {'dp','expert'}, dimensions={1} | all-to-all | bytes 7077888 | tf_op jit(solution)/shard_map/all_to_all | solution.py:53
  83.2 1.7 copy-done.3
  85.0 6.2 %fusion.12 = f32[2,1152,1024]{2,1,0:T(8,128)} fusion(bf16[2,1024,768]{2,1,0:T(8,128)(2,1)S(1)} %copy-done.11, bf16[2,1152,768]{2,0,1:T(2,128)(2,1)S(1)} %bitcast.56), kind=kOutput, calls=%fused_computation.24 | convolution fusion | flops 3623878656 | bytes 16121856 | tf_op jit(solution)/shard_map/esd,ehd->esh/dot_general | solution.py:55
  91.4 0.5 all-gather.2.cloned.1.call-update
  92.0 1.1 collective-permute-start
  93.0 11.5 %collective-permute-done = bf16[2,1152,128]{2,1,0:T(8,128)(2,1)S(1)} collective-permute-done((bf16[2,1152,128]{2,1,0:T(8,128)(2,1)}, bf16[2,1152,128]{2,1,0:T(8,128)(2,1)S(1)}, u32[]{:S(2)}, u32[]{:S(2)}) %collective-permute-start) | collective-permute-done | bytes 589856 | tf_op jit(solution)/shard_map/ppermute | solution.py:13
  104.5 0.8 copy-done.5
  105.4 2.4 collective-permute-start.1
  107.7 0.8 collective-permute-start.4
  108.5 12.5 %collective-permute-done.1 = bf16[2,1152,128]{2,1,0:T(8,128)(2,1)S(1)} collective-permute-done((bf16[2,1152,128]{2,1,0:T(8,128)(2,1)S(1)}, bf16[2,1152,128]{2,1,0:T(8,128)(2,1)S(1)}, u32[]{:S(2)}, u32[]{:S(2)}) %collective-permute-start.1) | collective-permute-done | bytes 589856 | tf_op jit(solution)/shard_map/ppermute | solution.py:13
  121.0 0.8 copy-done.7
  121.8 2.5 collective-permute-start.2
  124.3 2.0 collective-permute-start.5
  126.2 11.3 %collective-permute-done.2 = bf16[2,1152,128]{2,1,0:T(8,128)(2,1)} collective-permute-done((bf16[2,1152,128]{2,1,0:T(8,128)(2,1)S(1)}, bf16[2,1152,128]{2,1,0:T(8,128)(2,1)}, u32[]{:S(2)}, u32[]{:S(2)}) %collective-permute-start.2) | collective-permute-done | bytes 589856 | tf_op jit(solution)/shard_map/ppermute | solution.py:13
  137.5 2.6 collective-permute-start.3
  140.1 0.5 collective-permute-done.5
  140.6 2.7 collective-permute-start.6
  143.3 10.3 %collective-permute-done.3 = bf16[2,1152,128]{2,1,0:T(8,128)(2,1)} collective-permute-done((bf16[2,1152,128]{2,1,0:T(8,128)(2,1)}, bf16[2,1152,128]{2,1,0:T(8,128)(2,1)}, u32[]{:S(2)}, u32[]{:S(2)}) %collective-permute-start.3) | collective-permute-done | bytes 589856 | tf_op jit(solution)/shard_map/ppermute | solution.py:13
  153.6 2.0 constant_dynamic-update-slice_fusion.15
  155.6 2.1 constant_dynamic-update-slice_fusion.14
  157.7 2.0 constant_dynamic-update-slice_fusion.13
  159.7 2.0 constant_dynamic-update-slice_fusion.12
  161.7 2.0 constant_dynamic-update-slice_fusion.11
  163.7 2.0 constant_dynamic-update-slice_fusion.10
  165.7 2.0 constant_dynamic-update-slice_fusion.9
  167.7 0.9 constant_dynamic-update-slice_fusion.8
  168.5 2.0 constant_dynamic-update-slice_fusion.7
  170.5 2.0 constant_dynamic-update-slice_fusion.6
  172.6 0.9 constant_dynamic-update-slice_fusion.5
  173.5 0.9 constant_dynamic-update-slice_fusion.4
  174.4 0.9 constant_dynamic-update-slice_fusion.3
  175.3 2.1 constant_dynamic-update-slice_fusion.2
  177.4 2.0 constant_dynamic-update-slice_fusion.1
  179.4 0.9 constant_dynamic-update-slice_fusion
  180.4 39.7 %all-reduce.2.cloned.1.call-done = f32[2,1152,1024]{2,1,0:T(8,128)} async-done(((f32[2,1152,1024]{2,1,0:T(8,128)}), f32[2,1152,1024]{2,1,0:T(8,128)}) %all-reduce.2.cloned.1.call-update) | async-done | bytes 9437200 | tf_op jit(solution)/shard_map/psum | solution.py:58
  220.1 40.5 %all-gather.2.cloned.1.call-done = bf16[2,1152,1024]{2,1,0:T(8,128)(2,1)} async-done(((bf16[2,1152,128]{2,1,0:T(8,128)(2,1)}), bf16[2,1152,1024]{2,1,0:T(8,128)(2,1)}) %all-gather.2.cloned.1.call-update) | async-done | bytes 4718608 | tf_op jit(solution)/shard_map/all_gather | solution.py:60
  260.6 9.1 %fusion.2 = (bf16[2,1152,1024]{2,1,0:T(8,128)(2,1)S(1)}, bf16[2,1152,1024]{2,1,0:T(8,128)(2,1)S(1)}) fusion(f32[2,1152,1024]{2,1,0:T(8,128)} %all-reduce.2.cloned.1.call-done, bf16[2,1152,1024]{2,1,0:T(8,128)(2,1)} %all-gather.2.cloned.1.call-done, bf16[2,1152,2048]{2,1,0:T(8,128)(2,1)} %constant_dynamic-update-slice_fusion, s32[]{:T(128)S(6)} %select_n.35), kind=kLoop, calls=%fused_computation.7 | loop fusion | flops 35389440 | bytes 28311556 | tf_op jit(solution)/shard_map/convert_element_type | solution.py:68
  269.8 5.9 %fusion.32 = f32[2,1152,768]{2,1,0:T(8,128)} fusion(bf16[2,1152,1024]{2,1,0:T(8,128)(2,1)S(1)} %get-tuple-element.29, bf16[2,768,1024]{2,1,0:T(8,128)(2,1)S(1)} %copy-done.12), kind=kOutput, calls=%fused_computation.69 | convolution fusion | flops 3623878656 | bytes 14942208 | tf_op jit(solution)/shard_map/esh,edh->esd/dot_general | solution.py:81
  276.1 6.1 %add_convert_fusion = bf16[2,1152,768]{2,1,0:T(8,128)(2,1)S(1)} fusion(f32[2,1152,768]{2,1,0:T(8,128)} %fusion.32, bf16[2,1152,1024]{2,1,0:T(8,128)(2,1)S(1)} %get-tuple-element.28, bf16[2,768,1024]{2,1,0:T(8,128)(2,1)S(1)} %copy-done.13), kind=kOutput, calls=%fused_computation.16 | convolution fusion | flops 3627417600 | bytes 18481152 | tf_op jit(solution)/shard_map/esh,edh->esd/dot_general | solution.py:80
  282.2 14.0 %copy.112 = bf16[2,1152,768]{2,0,1:T(2,128)(2,1)} copy(bf16[2,1152,768]{2,1,0:T(8,128)(2,1)S(1)} %add_convert_fusion) | data formatting | bytes 7077888 | tf_op jit(solution)/shard_map/convert_element_type | solution.py:84
  296.2 9.3 %all-to-all-start.1 = ((bf16[2,128,9,768]{3,0,2,1:T(2,128)(2,1)}), bf16[2,128,9,768]{3,0,2,1:T(2,128)(2,1)}, u32[]{:S(2)}, u32[]{:S(2)}) async-start(bf16[2,128,9,768]{3,0,2,1:T(2,128)(2,1)} %bitcast.52), calls=%async_computation.1 | async-start | bytes 7077888 | tf_op jit(solution)/shard_map/all_to_all | solution.py:86
  305.5 9.4 %convert_bitcast_fusion.1 = bf16[2,768,1024]{1,2,0:T(8,128)(2,1)} fusion(bf16[2,1152,1024]{2,1,0:T(8,128)(2,1)} %copy-done.2, bf16[2,1152,768]{2,1,0:T(8,128)(2,1)S(1)} %copy-done), kind=kOutput, calls=%fused_computation.21 | convolution fusion | flops 3625451520 | bytes 11403264 | tf_op jit(solution)/shard_map/esd,esh->edh/dot_general | solution.py:74
  314.9 4.6 %copy.118 = bf16[2,768,1024]{2,1,0:T(8,128)(2,1)} copy(bf16[2,768,1024]{1,2,0:T(8,128)(2,1)} %convert_bitcast_fusion.1) | data formatting | bytes 6291456
  319.5 9.4 %convert_bitcast_fusion = bf16[2,768,1024]{1,2,0:T(8,128)(2,1)} fusion(bf16[2,1152,1024]{2,1,0:T(8,128)(2,1)} %copy-done.1, bf16[2,1152,768]{2,1,0:T(8,128)(2,1)S(1)} %copy-done), kind=kOutput, calls=%fused_computation.20 | convolution fusion | flops 3625451520 | bytes 11403264 | tf_op jit(solution)/shard_map/esd,esh->edh/dot_general | solution.py:77
  329.0 4.6 %copy.119 = bf16[2,768,1024]{2,1,0:T(8,128)(2,1)} copy(bf16[2,768,1024]{1,2,0:T(8,128)(2,1)} %convert_bitcast_fusion) | data formatting | bytes 6291456
  333.6 12.1 %fusion.14 = bf16[2,1024,768]{2,1,0:T(8,128)(2,1)} fusion(bf16[2,1152,768]{2,0,1:T(2,128)(2,1)} %bitcast.57, bf16[2,1152,2048]{2,1,0:T(8,128)(2,1)} %constant_dynamic-update-slice_fusion, s32[]{:T(128)S(6)} %select_n.35, bf16[2,1152,1024]{2,1,0:T(8,128)(2,1)} %all-gather.2.cloned.1.call-done), kind=kOutput, calls=%fused_computation.26 | convolution fusion | flops 3644325888 | bytes 16121860 | tf_op jit(solution)/shard_map/esh,esd->ehd/dot_general | solution.py:71
  345.8 5.4 %all-to-all-done.1 = bf16[2,128,9,768]{3,0,2,1:T(2,128)(2,1)} async-done(((bf16[2,128,9,768]{3,0,2,1:T(2,128)(2,1)}), bf16[2,128,9,768]{3,0,2,1:T(2,128)(2,1)}, u32[]{:S(2)}, u32[]{:S(2)}) %all-to-all-start.1) | async-done | bytes 3538976 | tf_op jit(solution)/shard_map/all_to_all | solution.py:86
  351.2 2.5 copy.113
  353.7 1.0 copy.125
  354.7 2.2 convolution_convert_fusion.1
  (34 shorter events, 1.2 us)
Async XLA Ops:
  7.2 298.3 %copy-start = (bf16[2,1152,768]{2,1,0:T(8,128)(2,1)S(1)}, bf16[2,1152,768]{2,1,0:T(8,128)(2,1)}, u32[]{:S(2)}) copy-start(bf16[2,1152,768]{2,1,0:T(8,128)(2,1)} %param.12) | copy-start | bytes 10616836
  7.2 212.9 %all-reduce.2.cloned.1.call-start = ((), (), s32[]{:S(2)}) async-start(), calls=%async_computation.2 | async-start | bytes 18874368 | tf_op jit(solution)/shard_map/psum | solution.py:58
  17.5 3.3 copy-start.9
  22.2 62.7 %copy-start.11 = (bf16[2,1024,768]{2,1,0:T(8,128)(2,1)S(1)}, bf16[2,1024,768]{2,1,0:T(8,128)(2,1)}, u32[]{:S(2)}) copy-start(bf16[2,1024,768]{2,1,0:T(8,128)(2,1)} %param.17) | copy-start | bytes 9437188
  83.2 1.7 copy-start.3
  91.2 169.4 %all-gather.2.cloned.1.call-start = ((), (), s32[]{:S(2)}) async-start(), calls=%async_computation.3 | async-start | bytes 5308416 | tf_op jit(solution)/shard_map/all_gather | solution.py:60
  92.0 12.6 %collective-permute-start = (bf16[2,1152,128]{2,1,0:T(8,128)(2,1)}, bf16[2,1152,128]{2,1,0:T(8,128)(2,1)S(1)}, u32[]{:S(2)}, u32[]{:S(2)}) collective-permute-start(bf16[2,1152,128]{2,1,0:T(8,128)(2,1)} %param.14), channel_id=1, source_target_pairs={{0,1},{1,2},{2,3},{3,4},{4,5},{5,6},{6,7},{7,0},{8,9},{9,10},{10,1... | collective-permute-start | bytes 1769480 | tf_op jit(solution)/shard_map/ppermute | solution.py:13
  104.5 0.8 copy-start.5
  105.4 15.6 %collective-permute-start.1 = (bf16[2,1152,128]{2,1,0:T(8,128)(2,1)S(1)}, bf16[2,1152,128]{2,1,0:T(8,128)(2,1)S(1)}, u32[]{:S(2)}, u32[]{:S(2)}) collective-permute-start(bf16[2,1152,128]{2,1,0:T(8,128)(2,1)S(1)} %collective-permute-done), channel_id=1, source_target_pairs={{0,1},{1,2},{2,3},{3,4},{4,5},{5,6},{6,7},{7,0},{8,9},{9,10},{10,1... | collective-permute-start | bytes 1769480 | tf_op jit(solution)/shard_map/ppermute | solution.py:13
  107.7 16.5 %collective-permute-start.4 = (bf16[2,1152,128]{2,1,0:T(8,128)(2,1)}, bf16[2,1152,128]{2,1,0:T(8,128)(2,1)}, u32[]{:S(2)}, u32[]{:S(2)}) collective-permute-start(bf16[2,1152,128]{2,1,0:T(8,128)(2,1)} %param.14), channel_id=1, source_target_pairs={{0,7},{1,0},{2,1},{3,2},{4,3},{5,4},{6,5},{7,6},{8,15},{9,8},{10,9... | collective-permute-start | bytes 1769480 | tf_op jit(solution)/shard_map/ppermute | solution.py:15
  121.0 0.8 copy-start.7
  121.8 15.7 %collective-permute-start.2 = (bf16[2,1152,128]{2,1,0:T(8,128)(2,1)S(1)}, bf16[2,1152,128]{2,1,0:T(8,128)(2,1)}, u32[]{:S(2)}, u32[]{:S(2)}) collective-permute-start(bf16[2,1152,128]{2,1,0:T(8,128)(2,1)S(1)} %collective-permute-done.1), channel_id=1, source_target_pairs={{0,1},{1,2},{2,3},{3,4},{4,5},{5,6},{6,7},{7,0},{8,9},{9,10},{10,1... | collective-permute-start | bytes 1769480 | tf_op jit(solution)/shard_map/ppermute | solution.py:13
  124.3 16.3 %collective-permute-start.5 = (bf16[2,1152,128]{2,1,0:T(8,128)(2,1)}, bf16[2,1152,128]{2,1,0:T(8,128)(2,1)}, u32[]{:S(2)}, u32[]{:S(2)}) collective-permute-start(bf16[2,1152,128]{2,1,0:T(8,128)(2,1)} %collective-permute-done.4), channel_id=1, source_target_pairs={{0,7},{1,0},{2,1},{3,2},{4,3},{5,4},{6,5},{7,6},{8,15},{9,8},{10,9... | collective-permute-start | bytes 1769480 | tf_op jit(solution)/shard_map/ppermute | solution.py:15
  137.5 16.1 %collective-permute-start.3 = (bf16[2,1152,128]{2,1,0:T(8,128)(2,1)}, bf16[2,1152,128]{2,1,0:T(8,128)(2,1)}, u32[]{:S(2)}, u32[]{:S(2)}) collective-permute-start(bf16[2,1152,128]{2,1,0:T(8,128)(2,1)} %collective-permute-done.2), channel_id=1, source_target_pairs={{0,1},{1,2},{2,3},{3,4},{4,5},{5,6},{6,7},{7,0},{8,9},{9,10},{10,1... | collective-permute-start | bytes 1769480 | tf_op jit(solution)/shard_map/ppermute | solution.py:13
  140.1 32.5 %copy-start.8 = (bf16[2,1152,128]{2,1,0:T(8,128)(2,1)S(1)}, bf16[2,1152,128]{2,1,0:T(8,128)(2,1)}, u32[]{:S(2)}) copy-start(bf16[2,1152,128]{2,1,0:T(8,128)(2,1)} %copy-done.7) | copy-start | bytes 1769476
  140.1 33.4 %copy-start.6 = (bf16[2,1152,128]{2,1,0:T(8,128)(2,1)S(1)}, bf16[2,1152,128]{2,1,0:T(8,128)(2,1)}, u32[]{:S(2)}) copy-start(bf16[2,1152,128]{2,1,0:T(8,128)(2,1)} %copy-done.5) | copy-start | bytes 1769476
  140.6 27.1 %collective-permute-start.6 = (bf16[2,1152,128]{2,1,0:T(8,128)(2,1)}, bf16[2,1152,128]{2,1,0:T(8,128)(2,1)S(1)}, u32[]{:S(2)}, u32[]{:S(2)}) collective-permute-start(bf16[2,1152,128]{2,1,0:T(8,128)(2,1)} %collective-permute-done.5), channel_id=1, source_target_pairs={{0,7},{1,0},{2,1},{3,2},{4,3},{5,4},{6,5},{7,6},{8,15},{9,8},{10,9... | collective-permute-start | bytes 1769480 | tf_op jit(solution)/shard_map/ppermute | solution.py:15
  155.6 18.8 %copy-start.4 = (bf16[2,1152,128]{2,1,0:T(8,128)(2,1)S(1)}, bf16[2,1152,128]{2,1,0:T(8,128)(2,1)}, u32[]{:S(2)}) copy-start(bf16[2,1152,128]{2,1,0:T(8,128)(2,1)} %param.14) | copy-start | bytes 1769476
  260.6 9.1 %copy-start.12 = (bf16[2,768,1024]{2,1,0:T(8,128)(2,1)S(1)}, bf16[2,768,1024]{2,1,0:T(8,128)(2,1)}, u32[]{:S(2)}) copy-start(bf16[2,768,1024]{2,1,0:T(8,128)(2,1)} %param.16) | copy-start | bytes 9437188
  269.7 6.0 %copy-start.1 = (bf16[2,1152,1024]{2,1,0:T(8,128)(2,1)}, bf16[2,1152,1024]{2,1,0:T(8,128)(2,1)S(1)}, u32[]{:S(2)}) copy-start(bf16[2,1152,1024]{2,1,0:T(8,128)(2,1)S(1)} %get-tuple-element.29) | copy-start | bytes 14155780
  269.7 6.4 %copy-start.2 = (bf16[2,1152,1024]{2,1,0:T(8,128)(2,1)}, bf16[2,1152,1024]{2,1,0:T(8,128)(2,1)S(1)}, u32[]{:S(2)}) copy-start(bf16[2,1152,1024]{2,1,0:T(8,128)(2,1)S(1)} %get-tuple-element.28) | copy-start | bytes 14155780
  269.7 6.4 %copy-start.13 = (bf16[2,768,1024]{2,1,0:T(8,128)(2,1)S(1)}, bf16[2,768,1024]{2,1,0:T(8,128)(2,1)}, u32[]{:S(2)}) copy-start(bf16[2,768,1024]{2,1,0:T(8,128)(2,1)} %param.15) | copy-start | bytes 9437188
  296.2 55.0 %all-to-all-start.1 = ((bf16[2,128,9,768]{3,0,2,1:T(2,128)(2,1)}), bf16[2,128,9,768]{3,0,2,1:T(2,128)(2,1)}, u32[]{:S(2)}, u32[]{:S(2)}) async-start(bf16[2,128,9,768]{3,0,2,1:T(2,128)(2,1)} %bitcast.52), calls=%async_computation.1 | async-start | bytes 7077888 | tf_op jit(solution)/shard_map/all_to_all | solution.py:86
  351.2 3.5 copy-start.10
Sparse Core Ops, SparseCore 0:
  91.3 128.7 all-reduce.1
  221.8 38.8 all-gather.1
